TPU v7x, 32 devices: a whole 2x2x4 slice. The times are simulated.
32 devices in a mesh: wide: 8 (over z, x), narrow: 4 (over y, core).
Axes of the slice: x: 2, y: 2, z: 4, core: 2. Of those that a mesh axis runs over, the one named last changes fastest.
Arguments:
- tokens: bfloat16 [2, 2, 1152, 8192], P(None, None, 'narrow', 'wide')
- ada_weight: bfloat16 [1152, 6, 1152], P('wide', None, 'narrow'), may hold values from -0.1875 to 0.1875
- ada_bias: bfloat16 [6, 1152], P(None, 'narrow'), may hold values from -3 to 3
- class_table: bfloat16 [101, 1152], replicated, may hold values from -6 to 6
- query_weight: bfloat16 [1152, 1152], P('wide', 'narrow'), may hold values from -0.1875 to 0.1875
- key_weight: bfloat16 [1152, 1152], P('wide', 'narrow'), may hold values from -0.1875 to 0.1875
- value_weight: bfloat16 [1152, 1152], P('wide', 'narrow'), may hold values from -0.1875 to 0.1875
- out_weight: bfloat16 [1152, 1152], P('narrow', 'wide'), may hold values from -0.375 to 0.375
- up_weight: bfloat16 [1152, 4608], P('wide', 'narrow')
- up_bias: bfloat16 [4608], P('narrow'), may hold values from -3 to 3
- down_weight: bfloat16 [4608, 1152], P('narrow', 'wide'), may hold values from -0.09375 to 0.09375
- down_bias: bfloat16 [1152], P('narrow'), may hold values from -3 to 3
- cotangent: bfloat16 [2, 2, 1152, 8192], P(None, None, 'narrow', 'wide'), may hold values from -6 to 6
- clip_frames: int32 [2, 2], replicated, may hold values from 1 to 16, as said below
- time_ids: int32 [2, 2], replicated, may hold values from 0 to 999
- class_ids: int32 [2, 2], replicated, may hold values from 0 to 100
Outputs:
- output: bfloat16 [2, 2, 1152, 8192], P(None, None, 'narrow', 'wide')
- input_grad: float32 [2, 2, 1152, 8192], P(None, None, 'narrow', 'wide')
- ada_weight_grad: float32 [1152, 6, 1152], P('wide', None, 'narrow')
- ada_bias_grad: float32 [6, 1152], P(None, 'narrow')
- class_table_grad: float32 [101, 1152], replicated
- query_weight_grad: float32 [1152, 1152], P('wide', 'narrow')
- key_weight_grad: float32 [1152, 1152], P('wide', 'narrow')
- value_weight_grad: float32 [1152, 1152], P('wide', 'narrow')
- out_weight_grad: float32 [1152, 1152], P('narrow', 'wide')
- up_weight_grad: float32 [1152, 4608], P('wide', 'narrow')
- up_bias_grad: float32 [4608], P('narrow')
- down_weight_grad: float32 [4608, 1152], P('narrow', 'wide')
- down_bias_grad: float32 [1152], P('narrow')
Inputs may be any that keep to these rules, and one draw needn't show every extreme that they name: Frames of a sequence at or after its clip_frames are single images. Some sequence of the first micro-batch is a clip of all 16 frames and some sequence of the last micro-batch has clip_frames 1.
All inputs are finite; a program needn't handle non-finite values.
Results may differ from a plain program's by a relative error of at most 0.02.
Values may be sent and summed in bfloat16 or wider, within the bound.
No kernel may reach another device: no remote copies, remote signals or barrier semaphores. Data moves between devices by JAX's collectives and lax.ppermute only.
A program may use at most 256 MiB of HBM per device.

v0:
```python
import math

import jax
import jax.numpy as jnp
from jax import lax
from jax.sharding import PartitionSpec as P

HEAD_DIM = 72
FRAMES = 16


norm_epsilon = 1e-06
masked_score = -1000000000.0


def time_embedding(time_ids, full_width):
    half_width = full_width // 2
    frequency = jnp.exp(-math.log(10000.0) * jnp.arange(half_width, dtype=jnp.float32) / half_width)
    angles = time_ids.astype(jnp.float32)[..., None] * frequency
    return jnp.concatenate([jnp.cos(angles), jnp.sin(angles)], axis=-1)


def gelu_tanh(values):
    return jax.nn.gelu(values, approximate=True)


def spread_features(normed_low):
    return lax.all_gather(normed_low, "narrow", axis=1, tiled=True)


def spread_grads(grads_low):
    return lax.all_gather(grads_low, "narrow", axis=1, tiled=True)


def reduce_columns(partial_value):
    return lax.psum_scatter(partial_value, "narrow", scatter_dimension=1, tiled=True)


def reduce_feature_grads(partial_value):
    return lax.psum_scatter(partial_value, "narrow", scatter_dimension=1, tiled=True)


def fetch_rows(ada_weight, query_weight, key_weight, value_weight, up_weight):
    return (
        lax.all_gather(ada_weight, "wide", axis=0, tiled=True),
        lax.all_gather(query_weight, "wide", axis=0, tiled=True),
        lax.all_gather(key_weight, "wide", axis=0, tiled=True),
        lax.all_gather(value_weight, "wide", axis=0, tiled=True),
        lax.all_gather(up_weight, "wide", axis=0, tiled=True),
    )


def fetch_columns(out_weight, down_weight):
    return (
        lax.all_gather(out_weight, "wide", axis=1, tiled=True),
        lax.all_gather(down_weight, "wide", axis=1, tiled=True),
    )


def norm_forward(residual, full_width):
    totals, squares = lax.psum(
        (jnp.sum(residual, axis=1), jnp.sum(residual * residual, axis=1)), "narrow"
    )
    center = totals / full_width
    variance = squares / full_width - center * center
    inverse = lax.rsqrt(variance + norm_epsilon)
    return ((residual - center[:, None, :]) * inverse[:, None, :], inverse)


def norm_backward(grad_hat, normed, inverse, full_width):
    totals, crossed = lax.psum(
        (jnp.sum(grad_hat, axis=1), jnp.sum(grad_hat * normed, axis=1)), "narrow"
    )
    return inverse[:, None, :] * (
        grad_hat - totals[:, None, :] / full_width - normed * (crossed[:, None, :] / full_width)
    )


def attention_scores(queries, key_rows, allowed, score_scale):
    raw_scores = (
        jnp.einsum("spfhc,spghc->sphfg", queries, key_rows, preferred_element_type=jnp.float32)
        * score_scale
    )
    return jnp.where(allowed, raw_scores, masked_score)


def on_device(
    tokens,
    ada_weight,
    ada_bias,
    class_table,
    query_weight,
    key_weight,
    value_weight,
    out_weight,
    up_weight,
    up_bias,
    down_weight,
    down_bias,
    cotangent,
    clip_frames,
    time_ids,
    class_ids,
):
    micro_count, seq_count, local_width, seq_tokens = tokens.shape
    class_count, full_width = class_table.shape
    frame_count = FRAMES
    patch_count = seq_tokens // frame_count
    head_dim = HEAD_DIM
    local_heads = local_width // head_dim
    score_scale = 1.0 / math.sqrt(head_dim)
    highest = lax.Precision.HIGHEST
    split_shape = (seq_count, patch_count, frame_count, local_heads, head_dim)
    flat_shape = (seq_count, seq_tokens, local_width)
    class_hot = (class_ids[..., None] == jnp.arange(class_count)[None, None, :]).astype(
        jnp.bfloat16
    )
    condition = time_embedding(time_ids, full_width) + jnp.einsum(
        "msc,cd->msd", class_hot, class_table, preferred_element_type=jnp.float32
    )
    sigmoid_cond = jax.nn.sigmoid(condition)
    cond_act = (condition * sigmoid_cond).astype(jnp.bfloat16)
    silu_slope = sigmoid_cond * (1.0 + condition * (1.0 - sigmoid_cond))
    frame_index = jnp.arange(frame_count)
    in_clip = frame_index[None, None, :] < clip_frames[:, :, None]
    allowed_all = (
        in_clip[..., :, None] & in_clip[..., None, :]
        | (frame_index[:, None] == frame_index[None, :])[None, None]
    )
    query_grad = jnp.zeros((full_width, local_width), jnp.float32)
    key_grad = jnp.zeros((full_width, local_width), jnp.float32)
    value_grad = jnp.zeros((full_width, local_width), jnp.float32)
    up_grad = jnp.zeros((full_width, up_weight.shape[1]), jnp.float32)
    out_grad = jnp.zeros((local_width, full_width), jnp.float32)
    down_grad = jnp.zeros((down_weight.shape[0], full_width), jnp.float32)
    up_bias_grad = jnp.zeros(up_bias.shape, jnp.float32)
    down_bias_grad = jnp.zeros(down_bias.shape, jnp.float32)
    outputs = []
    input_grads = []
    mod_grads = []
    for micro_index in range(micro_count):
        row_full = fetch_rows(ada_weight, query_weight, key_weight, value_weight, up_weight)
        column_full = fetch_columns(out_weight, down_weight)
        ada_full, query_full, key_full, value_full, up_full = row_full
        out_full, down_full = column_full
        modulation = jnp.einsum(
            "sd,dje->sje", cond_act[micro_index], ada_full, preferred_element_type=jnp.float32
        ) + ada_bias.astype(jnp.float32)
        shift_one, scale_one, gate_one, shift_two, scale_two, gate_two = [
            modulation[:, slot_index, :, None] for slot_index in range(6)
        ]
        residual = tokens[micro_index].astype(jnp.float32)
        normed_one, inverse_one = norm_forward(residual, full_width)
        input_one = spread_features(
            (normed_one * (1.0 + scale_one) + shift_one).astype(jnp.bfloat16)
        )
        queries = jnp.einsum(
            "sdl,de->sle", input_one, query_full, preferred_element_type=jnp.float32
        ).astype(jnp.bfloat16)
        key_rows = jnp.einsum(
            "sdl,de->sle", input_one, key_full, preferred_element_type=jnp.float32
        ).astype(jnp.bfloat16)
        value_rows = jnp.einsum(
            "sdl,de->sle", input_one, value_full, preferred_element_type=jnp.float32
        ).astype(jnp.bfloat16)
        query_heads = queries.reshape(split_shape)
        key_heads = key_rows.reshape(split_shape)
        value_heads = value_rows.reshape(split_shape)
        allowed = allowed_all[micro_index][:, None, None]
        scores = attention_scores(query_heads, key_heads, allowed, score_scale)
        score_peak = jnp.max(scores, axis=-1, keepdims=True)
        exp_scores = jnp.exp(scores - score_peak)
        exp_total = jnp.sum(exp_scores, axis=-1, keepdims=True)
        log_total = score_peak + jnp.log(exp_total)
        probs_low = (exp_scores / exp_total).astype(jnp.bfloat16)
        attended = (
            jnp.einsum(
                "sphfg,spghc->spfhc", probs_low, value_heads, preferred_element_type=jnp.float32
            )
            .astype(jnp.bfloat16)
            .reshape(flat_shape)
        )
        branch = reduce_columns(
            jnp.einsum("slh,hd->sdl", attended, out_full, preferred_element_type=jnp.float32)
        )
        middle = residual + gate_one * branch
        normed_two, inverse_two = norm_forward(middle, full_width)
        input_two = spread_features(
            (normed_two * (1.0 + scale_two) + shift_two).astype(jnp.bfloat16)
        )
        up_act = jnp.einsum(
            "sdl,df->slf", input_two, up_full, preferred_element_type=jnp.float32
        ) + up_bias.astype(jnp.float32)
        hidden_low = gelu_tanh(up_act).astype(jnp.bfloat16)
        mlp_out = (
            reduce_columns(
                jnp.einsum("slf,fd->sdl", hidden_low, down_full, preferred_element_type=jnp.float32)
            )
            + down_bias.astype(jnp.float32)[:, None]
        )
        outputs.append((middle + gate_two * mlp_out).astype(jnp.bfloat16))
        row_full = fetch_rows(ada_weight, query_weight, key_weight, value_weight, up_weight)
        column_full = fetch_columns(out_weight, down_weight)
        ada_full, query_full, key_full, value_full, up_full = row_full
        out_full, down_full = column_full
        upstream = cotangent[micro_index].astype(jnp.float32)
        grad_gate_two = jnp.sum(upstream * mlp_out, axis=2)
        grad_mlp = (gate_two * upstream).astype(jnp.bfloat16)
        down_bias_grad = down_bias_grad + jnp.sum(grad_mlp.astype(jnp.float32), axis=(0, 2))
        grad_mlp_full = spread_grads(grad_mlp)
        down_grad = down_grad + jnp.einsum(
            "slf,sdl->fd", hidden_low, grad_mlp_full, preferred_element_type=jnp.float32
        )
        grad_hidden = jnp.einsum(
            "sdl,fd->slf", grad_mlp_full, down_full, preferred_element_type=jnp.float32
        )
        grad_up = jax.vjp(gelu_tanh, up_act)[1](grad_hidden)[0].astype(jnp.bfloat16)
        up_bias_grad = up_bias_grad + jnp.sum(grad_up.astype(jnp.float32), axis=(0, 1))
        up_grad = up_grad + jnp.einsum(
            "sdl,slf->df", input_two, grad_up, preferred_element_type=jnp.float32
        )
        grad_input_two = reduce_feature_grads(
            jnp.einsum("slf,df->sdl", grad_up, up_full, preferred_element_type=jnp.float32)
        )
        grad_shift_two = jnp.sum(grad_input_two, axis=2)
        grad_scale_two = jnp.sum(grad_input_two * normed_two, axis=2)
        grad_middle = upstream + norm_backward(
            grad_input_two * (1.0 + scale_two), normed_two, inverse_two, full_width
        )
        grad_gate_one = jnp.sum(grad_middle * branch, axis=2)
        grad_branch_full = spread_grads((gate_one * grad_middle).astype(jnp.bfloat16))
        out_grad = out_grad + jnp.einsum(
            "slh,sdl->hd", attended, grad_branch_full, preferred_element_type=jnp.float32
        )
        grad_attended = (
            jnp.einsum(
                "sdl,hd->slh", grad_branch_full, out_full, preferred_element_type=jnp.float32
            )
            .astype(jnp.bfloat16)
            .reshape(split_shape)
        )
        again_scores = attention_scores(query_heads, key_heads, allowed, score_scale)
        prob_rows = jnp.exp(again_scores - log_total)
        prob_rows_low = prob_rows.astype(jnp.bfloat16)
        grad_probs = jnp.einsum(
            "spfhc,spghc->sphfg", grad_attended, value_heads, preferred_element_type=jnp.float32
        )
        grad_values = (
            jnp.einsum(
                "sphfg,spfhc->spghc",
                prob_rows_low,
                grad_attended,
                preferred_element_type=jnp.float32,
            )
            .astype(jnp.bfloat16)
            .reshape(flat_shape)
        )
        grad_scores = (
            prob_rows * (grad_probs - jnp.sum(grad_probs * prob_rows, axis=-1, keepdims=True))
        ).astype(jnp.bfloat16)
        grad_queries = (
            (
                jnp.einsum(
                    "sphfg,spghc->spfhc", grad_scores, key_heads, preferred_element_type=jnp.float32
                )
                * score_scale
            )
            .astype(jnp.bfloat16)
            .reshape(flat_shape)
        )
        grad_keys = (
            (
                jnp.einsum(
                    "sphfg,spfhc->spghc",
                    grad_scores,
                    query_heads,
                    preferred_element_type=jnp.float32,
                )
                * score_scale
            )
            .astype(jnp.bfloat16)
            .reshape(flat_shape)
        )
        query_grad = query_grad + jnp.einsum(
            "sdl,slh->dh", input_one, grad_queries, preferred_element_type=jnp.float32
        )
        key_grad = key_grad + jnp.einsum(
            "sdl,slh->dh", input_one, grad_keys, preferred_element_type=jnp.float32
        )
        value_grad = value_grad + jnp.einsum(
            "sdl,slh->dh", input_one, grad_values, preferred_element_type=jnp.float32
        )
        input_partial = jnp.einsum(
            "slh,dh->sdl", grad_queries, query_full, preferred_element_type=jnp.float32
        )
        input_partial = input_partial + jnp.einsum(
            "slh,dh->sdl", grad_keys, key_full, preferred_element_type=jnp.float32
        )
        input_partial = input_partial + jnp.einsum(
            "slh,dh->sdl", grad_values, value_full, preferred_element_type=jnp.float32
        )
        grad_input_one = reduce_feature_grads(input_partial)
        grad_shift_one = jnp.sum(grad_input_one, axis=2)
        grad_scale_one = jnp.sum(grad_input_one * normed_one, axis=2)
        grad_tokens = grad_middle + norm_backward(
            grad_input_one * (1.0 + scale_one), normed_one, inverse_one, full_width
        )
        input_grads.append(grad_tokens)
        mod_grads.append(
            jnp.stack(
                [
                    grad_shift_one,
                    grad_scale_one,
                    grad_gate_one,
                    grad_shift_two,
                    grad_scale_two,
                    grad_gate_two,
                ],
                axis=1,
            )
        )
    mod_grad = jnp.stack(mod_grads)
    cond_wide = cond_act.astype(jnp.float32)
    ada_cast = ada_full.astype(jnp.float32)
    ada_local = jnp.einsum("msd,msje->dje", cond_wide, mod_grad, precision=highest)
    ada_bias_local = jnp.sum(mod_grad, axis=(0, 1))
    cond_local = silu_slope * jnp.einsum("msje,dje->msd", mod_grad, ada_cast, precision=highest)
    up_bias_grad, down_bias_grad, ada_bias_grad, cond_part = lax.psum(
        (up_bias_grad, down_bias_grad, ada_bias_local, cond_local), "wide"
    )
    ada_grad, query_grad, key_grad, value_grad, up_grad = (
        lax.psum_scatter(ada_local, "wide", scatter_dimension=0, tiled=True),
        lax.psum_scatter(query_grad, "wide", scatter_dimension=0, tiled=True),
        lax.psum_scatter(key_grad, "wide", scatter_dimension=0, tiled=True),
        lax.psum_scatter(value_grad, "wide", scatter_dimension=0, tiled=True),
        lax.psum_scatter(up_grad, "wide", scatter_dimension=0, tiled=True),
    )
    out_grad, down_grad = (
        lax.psum_scatter(out_grad, "wide", scatter_dimension=1, tiled=True),
        lax.psum_scatter(down_grad, "wide", scatter_dimension=1, tiled=True),
    )
    cond_grad = lax.psum(cond_part, "narrow")
    table_grad = jnp.einsum(
        "msc,msd->cd", class_hot.astype(jnp.float32), cond_grad, precision=highest
    )
    return (
        jnp.stack(outputs),
        jnp.stack(input_grads),
        ada_grad,
        ada_bias_grad,
        table_grad,
        query_grad,
        key_grad,
        value_grad,
        out_grad,
        up_grad,
        up_bias_grad,
        down_grad,
        down_bias_grad,
    )


def solution(mesh):
    return jax.shard_map(
        on_device,
        mesh=mesh,
        in_specs=(
            P(None, None, "narrow", "wide"),
            P("wide", None, "narrow"),
            P(None, "narrow"),
            P(),
            P("wide", "narrow"),
            P("wide", "narrow"),
            P("wide", "narrow"),
            P("narrow", "wide"),
            P("wide", "narrow"),
            P("narrow"),
            P("narrow", "wide"),
            P("narrow"),
            P(None, None, "narrow", "wide"),
            P(),
            P(),
            P(),
        ),
        out_specs=(
            P(None, None, "narrow", "wide"),
            P(None, None, "narrow", "wide"),
            P("wide", None, "narrow"),
            P(None, "narrow"),
            P(),
            P("wide", "narrow"),
            P("wide", "narrow"),
            P("wide", "narrow"),
            P("narrow", "wide"),
            P("wide", "narrow"),
            P("narrow"),
            P("narrow", "wide"),
            P("narrow"),
        ),
        check_vma=False,
    )
```

profile of v0, /device:TPU:0, one launch (start us, length us, event | category | flops | bytes accessed | tf_op | source)
XLA Modules:
  0.0 2309.1 jit_solution(13515034563534353171)
XLA Ops:
  13.0 12.7 all-reduce.7
  26.8 73.3 %all-gather.12.cloned.1.call-done = bf16[1152,6,288]{2,0,1:T(8,128)(2,1)} async-done(((bf16[144,6,288]{2,0,1:T(8,128)(2,1)}), bf16[1152,6,288]{2,0,1:T(8,128)(2,1)}) %all-gather.12.cloned.1.call-update) | async-done | bytes 3981328 | tf_op jit(solution)/shard_map/all_gather | solution.py:45
  105.9 32.8 %all_gather.33 = bf16[1152,288]{1,0:T(8,128)(2,1)S(1)} all-gather(bf16[144,288]{1,0:T(8,128)(2,1)S(1)} %copy-done.55), channel_id=1, replica_groups=mesh['wide'=8,'narrow'=4] {'wide'}, dimensions={0}, use_global_device_ids=true | all-gather | bytes 746496 | tf_op jit(solution)/shard_map/all_gather | solution.py:46
  138.7 34.4 %all_gather.34 = bf16[1152,288]{1,0:T(8,128)(2,1)} all-gather(bf16[144,288]{1,0:T(8,128)(2,1)S(1)} %copy-done.56), channel_id=1, replica_groups=mesh['wide'=8,'narrow'=4] {'wide'}, dimensions={0}, use_global_device_ids=true | all-gather | bytes 746496 | tf_op jit(solution)/shard_map/all_gather | solution.py:47
  173.1 35.1 %all_gather.32 = bf16[1152,288]{1,0:T(8,128)(2,1)} all-gather(bf16[144,288]{1,0:T(8,128)(2,1)} %param.22), channel_id=1, replica_groups=mesh['wide'=8,'narrow'=4] {'wide'}, dimensions={0}, use_global_device_ids=true | all-gather | bytes 746496 | tf_op jit(solution)/shard_map/all_gather | solution.py:48
  208.2 34.4 %all_gather.70 = bf16[288,1152]{0,1:T(8,128)(2,1)} all-gather(bf16[288,144]{0,1:T(8,128)(2,1)} %param.23), channel_id=1, replica_groups=mesh['wide'=8,'narrow'=4] {'wide'}, dimensions={1}, use_global_device_ids=true | all-gather | bytes 746496 | tf_op jit(solution)/shard_map/all_gather | solution.py:55
  305.5 75.3 %reduce-scatter.16.cloned.1.call-done = f32[2,288,1024]{2,1,0:T(8,128)} async-done(((f32[2,1152,1024]{2,1,0:T(8,128)}), f32[2,288,1024]{2,1,0:T(8,128)}) %reduce-scatter.16.cloned.1.call-update) | async-done | bytes 2359312 | tf_op jit(solution)/shard_map/reduce_scatter | solution.py:36
  384.4 10.1 all-reduce.6
  401.6 36.2 %all-gather.18.cloned.1.call-done = bf16[1152,1152]{1,0:T(8,128)(2,1)} async-done(((bf16[144,1152]{1,0:T(8,128)(2,1)}), bf16[1152,1152]{1,0:T(8,128)(2,1)}) %all-gather.18.cloned.1.call-update) | async-done | bytes 2654224 | tf_op jit(solution)/shard_map/all_gather | solution.py:49
  437.8 38.1 %all-gather.16.cloned.1.call-done = bf16[2,1152,1024]{2,1,0:T(8,128)(2,1)} async-done(((bf16[2,288,1024]{2,1,0:T(8,128)(2,1)}), bf16[2,1152,1024]{2,1,0:T(8,128)(2,1)}) %all-gather.16.cloned.1.call-update) | async-done | bytes 4718608 | tf_op jit(solution)/shard_map/all_gather | solution.py:28
  475.9 11.8 fusion.40
  487.7 45.3 %all-gather.20.cloned.1.call-done = bf16[1152,1152]{0,1:T(8,128)(2,1)} async-done(((bf16[1152,144]{0,1:T(8,128)(2,1)}), bf16[1152,1152]{0,1:T(8,128)(2,1)}) %all-gather.20.cloned.1.call-update) | async-done | bytes 2654224 | tf_op jit(solution)/shard_map/all_gather | solution.py:56
  533.0 38.2 %all-gather.26.cloned.1.call-done = bf16[2,1152,1024]{2,1,0:T(8,128)(2,1)} async-done(((bf16[2,288,1024]{2,1,0:T(8,128)(2,1)}), bf16[2,1152,1024]{2,1,0:T(8,128)(2,1)}) %all-gather.26.cloned.1.call-update) | async-done | bytes 4718608 | tf_op jit(solution)/shard_map/all_gather | solution.py:32
  571.2 17.8 convert_reduce_fusion.1
  591.2 9.2 convolution_bitcast_fusion.6
  603.8 75.2 %reduce-scatter.24.cloned.1.call-done = f32[2,288,1024]{2,1,0:T(8,128)} async-done(((f32[2,1152,1024]{2,1,0:T(8,128)}), f32[2,288,1024]{2,1,0:T(8,128)}) %reduce-scatter.24.cloned.1.call-update) | async-done | bytes 2359312 | tf_op jit(solution)/shard_map/reduce_scatter | solution.py:40
  682.9 10.1 all-reduce.5
  703.4 36.8 %all-gather.28.cloned.1.call-done = bf16[2,1152,1024]{2,1,0:T(8,128)(2,1)} async-done(((bf16[2,288,1024]{2,1,0:T(8,128)(2,1)}), bf16[2,1152,1024]{2,1,0:T(8,128)(2,1)}) %all-gather.28.cloned.1.call-update) | async-done | bytes 4718608 | tf_op jit(solution)/shard_map/all_gather | solution.py:32
  803.8 78.4 %reduce-scatter.26.cloned.1.call-done = f32[2,288,1024]{2,1,0:T(8,128)} async-done(((f32[2,1152,1024]{2,1,0:T(8,128)}), f32[2,288,1024]{2,1,0:T(8,128)}) %reduce-scatter.26.cloned.1.call-update) | async-done | bytes 2359312 | tf_op jit(solution)/shard_map/reduce_scatter | solution.py:40
  885.7 10.1 all-reduce.4
  897.5 38.6 %all-gather.22.cloned.1.call-done = bf16[2,1152,1024]{2,1,0:T(8,128)(2,1)} async-done(((bf16[2,288,1024]{2,1,0:T(8,128)(2,1)}), bf16[2,1152,1024]{2,1,0:T(8,128)(2,1)}) %all-gather.22.cloned.1.call-update) | async-done | bytes 4718608 | tf_op jit(solution)/shard_map/all_gather | solution.py:28
  998.0 78.5 %reduce-scatter.20.cloned.1.call-done = f32[2,288,1024]{2,1,0:T(8,128)} async-done(((f32[2,1152,1024]{2,1,0:T(8,128)}), f32[2,288,1024]{2,1,0:T(8,128)}) %reduce-scatter.20.cloned.1.call-update) | async-done | bytes 2359312 | tf_op jit(solution)/shard_map/reduce_scatter | solution.py:36
  1080.1 10.1 all-reduce.3
  1094.0 38.0 %all-gather.24.cloned.1.call-done = bf16[2,1152,1024]{2,1,0:T(8,128)(2,1)} async-done(((bf16[2,288,1024]{2,1,0:T(8,128)(2,1)}), bf16[2,1152,1024]{2,1,0:T(8,128)(2,1)}) %all-gather.24.cloned.1.call-update) | async-done | bytes 4718608 | tf_op jit(solution)/shard_map/all_gather | solution.py:28
  1132.1 12.1 fusion.38
  1144.2 27.3 %all-gather.30.cloned.1.call-done = bf16[2,1152,1024]{2,1,0:T(8,128)(2,1)} async-done(((bf16[2,288,1024]{2,1,0:T(8,128)(2,1)}), bf16[2,1152,1024]{2,1,0:T(8,128)(2,1)}) %all-gather.30.cloned.1.call-update) | async-done | bytes 4718608 | tf_op jit(solution)/shard_map/all_gather | solution.py:32
  1171.6 17.8 convert_reduce_fusion
  1191.6 8.9 convolution_bitcast_fusion.5
  1200.6 12.9 convolution_bitcast_fusion.9
  1213.5 13.3 convolution_bitcast_fusion.7
  1227.5 51.6 %reduce-scatter.28.cloned.1.call-done = f32[2,288,1024]{2,1,0:T(8,128)} async-done(((f32[2,1152,1024]{2,1,0:T(8,128)}), f32[2,288,1024]{2,1,0:T(8,128)}) %reduce-scatter.28.cloned.1.call-update) | async-done | bytes 2359312 | tf_op jit(solution)/shard_map/reduce_scatter | solution.py:40
  1282.4 10.1 all-reduce.2
  1292.6 67.4 %reduce-scatter.18.cloned.1.call-done = f32[2,288,1024]{2,1,0:T(8,128)} async-done(((f32[2,1152,1024]{2,1,0:T(8,128)}), f32[2,288,1024]{2,1,0:T(8,128)}) %reduce-scatter.18.cloned.1.call-update) | async-done | bytes 2359312 | tf_op jit(solution)/shard_map/reduce_scatter | solution.py:36
  1360.0 80.9 %reduce-scatter.22.cloned.1.call-done = f32[2,288,1024]{2,1,0:T(8,128)} async-done(((f32[2,1152,1024]{2,1,0:T(8,128)}), f32[2,288,1024]{2,1,0:T(8,128)}) %reduce-scatter.22.cloned.1.call-update) | async-done | bytes 2359312 | tf_op jit(solution)/shard_map/reduce_scatter | solution.py:36
  1451.1 37.5 %all-gather.32.cloned.1.call-done = bf16[2,1152,1024]{2,1,0:T(8,128)(2,1)} async-done(((bf16[2,288,1024]{2,1,0:T(8,128)(2,1)}), bf16[2,1152,1024]{2,1,0:T(8,128)(2,1)}) %all-gather.32.cloned.1.call-update) | async-done | bytes 4718608 | tf_op jit(solution)/shard_map/all_gather | solution.py:32
  1544.7 11.8 convolution_bitcast_fusion.1
  1556.5 16.0 fusion.14
  1572.6 9.8 convolution_bitcast_fusion.3
  1582.3 11.1 fusion.15
  1662.8 39.7 %all-reduce = (f32[6,288]{1,0:T(8,128)}, f32[2,2,1152]{2,1,0:T(2,128)S(1)}, f32[1152]{0:T(1024)}, f32[288]{0:T(512)}) all-reduce(f32[6,288]{1,0:T(8,128)S(1)} %reduce_sum.375, f32[2,2,1152]{2,1,0:T(2,128)S(1)} %fusion.77, f32[1152]{0:T(1024)S(1)} %add.386, f32[288]{0:T(512)S(1)} %add.388), channel_id=1, replica_groups=mesh['wide'=8,'narrow'=4] {'wide'}, use_global_device_ids=true, to_apply=%region_61.62 | all-reduce | flops 7776 | bytes 62208 | tf_op jit(solution)/shard_map/psum | solution.py:328
  1702.4 11.0 all-reduce.1
  1722.3 10.6 reduce-scatter.44.cloned.1.call-done
  1733.0 108.6 %reduce-scatter.42.cloned.1.call-done = f32[144,1152]{1,0:T(8,128)} async-done(((f32[1152,1152]{1,0:T(8,128)}), f32[144,1152]{1,0:T(8,128)}) %reduce-scatter.42.cloned.1.call-update) | async-done | bytes 663568 | tf_op jit(solution)/shard_map/reduce_scatter | solution.py:336
  1841.5 69.8 %reduce-scatter.40.cloned.1.call-done = f32[288,144]{0,1:T(8,128)} async-done(((f32[288,1152]{0,1:T(8,128)}), f32[288,144]{0,1:T(8,128)}) %reduce-scatter.40.cloned.1.call-update) | async-done | bytes 165904 | tf_op jit(solution)/shard_map/reduce_scatter | solution.py:339
  1911.4 69.4 %reduce-scatter.38.cloned.1.call-done = f32[144,288]{1,0:T(8,128)} async-done(((f32[1152,288]{1,0:T(8,128)}), f32[144,288]{1,0:T(8,128)}) %reduce-scatter.38.cloned.1.call-update) | async-done | bytes 165904 | tf_op jit(solution)/shard_map/reduce_scatter | solution.py:335
  1980.8 69.1 %reduce-scatter.36.cloned.1.call-done = f32[144,288]{1,0:T(8,128)} async-done(((f32[1152,288]{1,0:T(8,128)}), f32[144,288]{1,0:T(8,128)}) %reduce-scatter.36.cloned.1.call-update) | async-done | bytes 165904 | tf_op jit(solution)/shard_map/reduce_scatter | solution.py:334
  2049.9 69.6 %reduce-scatter.34.cloned.1.call-done = f32[144,288]{1,0:T(8,128)} async-done(((f32[1152,288]{1,0:T(8,128)}), f32[144,288]{1,0:T(8,128)}) %reduce-scatter.34.cloned.1.call-update) | async-done | bytes 165904 | tf_op jit(solution)/shard_map/reduce_scatter | solution.py:333
  2119.5 182.9 %reduce-scatter.32.cloned.1.call-done = f32[144,6,288]{2,0,1:T(8,128)} async-done(((f32[1152,6,288]{2,0,1:T(8,128)}), f32[144,6,288]{2,0,1:T(8,128)}) %reduce-scatter.32.cloned.1.call-update) | async-done | bytes 995344 | tf_op jit(solution)/shard_map/reduce_scatter | solution.py:332
  (372 shorter events, 393.5 us)
Async XLA Ops:
  7.2 92.9 %all-gather.12.cloned.1.call-start = ((), (), s32[]{:S(2)}) async-start(), calls=%async_computation.15 | async-start | bytes 5971968 | tf_op jit(solution)/shard_map/all_gather | solution.py:45
  7.9 234.7 %all-gather.14.cloned.1.call-start = ((), (), s32[]{:S(2)}) async-start(), calls=%async_computation.16 | async-start | bytes 5898240 | tf_op jit(solution)/shard_map/all_gather | solution.py:28
  25.9 856.3 %copy-start.47 = (f32[2,1024]{1,0:T(2,128)}, f32[2,1024]{1,0:T(2,128)S(1)}, u32[]{:S(2)}) copy-start(f32[2,1024]{1,0:T(2,128)S(1)} %get-tuple-element.95) | copy-start | bytes 24580
  25.9 856.3 %copy-start.49 = (f32[2,1024]{1,0:T(2,128)}, f32[2,1024]{1,0:T(2,128)S(1)}, u32[]{:S(2)}) copy-start(f32[2,1024]{1,0:T(2,128)S(1)} %get-tuple-element.96) | copy-start | bytes 24580
  26.8 573.7 %copy-start.61 = (bf16[2,2,1152]{2,1,0:T(2,128)(2,1)}, bf16[2,2,1152]{2,1,0:T(2,128)(2,1)S(1)}, u32[]{:S(2)}) copy-start(bf16[2,2,1152]{2,1,0:T(2,128)(2,1)S(1)} %get-tuple-element.101) | copy-start | bytes 27652
  103.5 35.2 %copy-start.56 = (bf16[144,288]{1,0:T(8,128)(2,1)S(1)}, bf16[144,288]{1,0:T(8,128)(2,1)}, u32[]{:S(2)}) copy-start(bf16[144,288]{1,0:T(8,128)(2,1)} %param.21) | copy-start | bytes 248836
  103.6 294.7 %copy-start.67 = (f32[2,288]{1,0:T(2,128)}, f32[2,288]{1,0:T(2,128)S(1)}, u32[]{:S(2)}) copy-start(f32[2,288]{1,0:T(2,128)S(1)} %get-tuple-element.85) | copy-start | bytes 6916
  103.6 778.7 %copy-start.59 = (f32[2,288]{1,0:T(2,128)}, f32[2,288]{1,0:T(2,128)S(1)}, u32[]{:S(2)}) copy-start(f32[2,288]{1,0:T(2,128)S(1)} %get-tuple-element.87) | copy-start | bytes 6916
  105.1 275.7 %reduce-scatter.16.cloned.1.call-start = ((), (), s32[]{:S(2)}) async-start(), calls=%async_computation.17 | async-start | bytes 11796480 | tf_op jit(solution)/shard_map/reduce_scatter | solution.py:36
  138.7 810.7 %copy-start.20 = (bf16[1152,288]{1,0:T(8,128)(2,1)}, bf16[1152,288]{1,0:T(8,128)(2,1)S(1)}, u32[]{:S(2)}) copy-start(bf16[1152,288]{1,0:T(8,128)(2,1)S(1)} %all_gather.33) | copy-start | bytes 1990660
  304.8 133.0 %all-gather.18.cloned.1.call-start = ((), (), s32[]{:S(2)}) async-start(), calls=%async_computation.19 | async-start | bytes 2985984 | tf_op jit(solution)/shard_map/all_gather | solution.py:49
  305.4 170.5 %all-gather.16.cloned.1.call-start = ((), (), s32[]{:S(2)}) async-start(), calls=%async_computation.18 | async-start | bytes 5898240 | tf_op jit(solution)/shard_map/all_gather | solution.py:28
  397.7 135.3 %all-gather.20.cloned.1.call-start = ((), (), s32[]{:S(2)}) async-start(), calls=%async_computation.20 | async-start | bytes 2985984 | tf_op jit(solution)/shard_map/all_gather | solution.py:56
  398.2 173.0 %all-gather.26.cloned.1.call-start = ((), (), s32[]{:S(2)}) async-start(), calls=%async_computation.26 | async-start | bytes 5898240 | tf_op jit(solution)/shard_map/all_gather | solution.py:32
  401.5 277.5 %reduce-scatter.24.cloned.1.call-start = ((), (), s32[]{:S(2)}) async-start(), calls=%async_computation.27 | async-start | bytes 11796480 | tf_op jit(solution)/shard_map/reduce_scatter | solution.py:40
  571.2 20.0 copy-start.85
  600.4 139.8 %all-gather.28.cloned.1.call-start = ((), (), s32[]{:S(2)}) async-start(), calls=%async_computation.28 | async-start | bytes 5898240 | tf_op jit(solution)/shard_map/all_gather | solution.py:32
  603.8 89.3 %copy-start.65 = (f32[2,288]{1,0:T(2,128)}, f32[2,288]{1,0:T(2,128)S(1)}, u32[]{:S(2)}) copy-start(f32[2,288]{1,0:T(2,128)S(1)} %get-tuple-element.77) | copy-start | bytes 6916
  603.8 292.1 %copy-start.57 = (f32[2,288]{1,0:T(2,128)}, f32[2,288]{1,0:T(2,128)S(1)}, u32[]{:S(2)}) copy-start(f32[2,288]{1,0:T(2,128)S(1)} %get-tuple-element.81) | copy-start | bytes 6916
  701.6 180.7 %reduce-scatter.26.cloned.1.call-start = ((), (), s32[]{:S(2)}) async-start(), calls=%async_computation.29 | async-start | bytes 11796480 | tf_op jit(solution)/shard_map/reduce_scatter | solution.py:40
  803.8 132.3 %all-gather.22.cloned.1.call-start = ((), (), s32[]{:S(2)}) async-start(), calls=%async_computation.22 | async-start | bytes 5898240 | tf_op jit(solution)/shard_map/all_gather | solution.py:28
  895.9 45.5 %copy-start.51 = (f32[2,1024]{1,0:T(2,128)}, f32[2,1024]{1,0:T(2,128)S(1)}, u32[]{:S(2)}) copy-start(f32[2,1024]{1,0:T(2,128)S(1)} %get-tuple-element.91) | copy-start | bytes 24580
  895.9 45.5 %copy-start.53 = (f32[2,1024]{1,0:T(2,128)}, f32[2,1024]{1,0:T(2,128)S(1)}, u32[]{:S(2)}) copy-start(f32[2,1024]{1,0:T(2,128)S(1)} %get-tuple-element.92) | copy-start | bytes 24580
  897.4 179.1 %reduce-scatter.20.cloned.1.call-start = ((), (), s32[]{:S(2)}) async-start(), calls=%async_computation.23 | async-start | bytes 11796480 | tf_op jit(solution)/shard_map/reduce_scatter | solution.py:36
  998.0 134.1 %all-gather.24.cloned.1.call-start = ((), (), s32[]{:S(2)}) async-start(), calls=%async_computation.24 | async-start | bytes 5898240 | tf_op jit(solution)/shard_map/all_gather | solution.py:28
  1093.4 78.2 %all-gather.30.cloned.1.call-start = ((), (), s32[]{:S(2)}) async-start(), calls=%async_computation.30 | async-start | bytes 5898240 | tf_op jit(solution)/shard_map/all_gather | solution.py:32
  1094.0 185.1 %reduce-scatter.28.cloned.1.call-start = ((), (), s32[]{:S(2)}) async-start(), calls=%async_computation.31 | async-start | bytes 11796480 | tf_op jit(solution)/shard_map/reduce_scatter | solution.py:40
  1200.5 159.5 %reduce-scatter.18.cloned.1.call-start = ((), (), s32[]{:S(2)}) async-start(), calls=%async_computation.21 | async-start | bytes 11796480 | tf_op jit(solution)/shard_map/reduce_scatter | solution.py:36
  1213.5 227.5 %reduce-scatter.22.cloned.1.call-start = ((), (), s32[]{:S(2)}) async-start(), calls=%async_computation.25 | async-start | bytes 11796480 | tf_op jit(solution)/shard_map/reduce_scatter | solution.py:36
  1226.8 261.7 %all-gather.32.cloned.1.call-start = ((), (), s32[]{:S(2)}) async-start(), calls=%async_computation.32 | async-start | bytes 5898240 | tf_op jit(solution)/shard_map/all_gather | solution.py:32
  1227.5 213.4 %copy-start.8 = (f32[2,288,1024]{2,1,0:T(8,128)S(1)}, f32[2,288,1024]{2,1,0:T(8,128)}, u32[]{:S(2)}) copy-start(f32[2,288,1024]{2,1,0:T(8,128)} %get-tuple-element.68) | copy-start | bytes 7077892
  1227.5 213.4 %copy-start.66 = (f32[2,288]{1,0:T(2,128)S(1)}, f32[2,288]{1,0:T(2,128)}, u32[]{:S(2)}) copy-start(f32[2,288]{1,0:T(2,128)} %copy-done.65) | copy-start | bytes 6916
  1227.5 213.4 %copy-start.68 = (f32[2,288]{1,0:T(2,128)S(1)}, f32[2,288]{1,0:T(2,128)}, u32[]{:S(2)}) copy-start(f32[2,288]{1,0:T(2,128)} %copy-done.67) | copy-start | bytes 6916
  1451.0 190.8 %reduce-scatter.30.cloned.1.call-start = ((), (), s32[]{:S(2)}) async-start(), calls=%async_computation.33 | async-start | bytes 11796480 | tf_op jit(solution)/shard_map/reduce_scatter | solution.py:40
  1544.6 188.3 %reduce-scatter.44.cloned.1.call-start = ((), (), s32[]{:S(2)}) async-start(), calls=%async_computation.40 | async-start | bytes 5971968 | tf_op jit(solution)/shard_map/reduce_scatter | solution.py:340
  1572.5 269.0 %reduce-scatter.42.cloned.1.call-start = ((), (), s32[]{:S(2)}) async-start(), calls=%async_computation.39 | async-start | bytes 5971968 | tf_op jit(solution)/shard_map/reduce_scatter | solution.py:336
  1593.4 317.9 %reduce-scatter.40.cloned.1.call-start = ((), (), s32[]{:S(2)}) async-start(), calls=%async_computation.38 | async-start | bytes 1990656 | tf_op jit(solution)/shard_map/reduce_scatter | solution.py:339
  1606.3 374.5 %reduce-scatter.38.cloned.1.call-start = ((), (), s32[]{:S(2)}) async-start(), calls=%async_computation.37 | async-start | bytes 1990656 | tf_op jit(solution)/shard_map/reduce_scatter | solution.py:335
  1618.2 431.7 %reduce-scatter.36.cloned.1.call-start = ((), (), s32[]{:S(2)}) async-start(), calls=%async_computation.36 | async-start | bytes 1990656 | tf_op jit(solution)/shard_map/reduce_scatter | solution.py:334
  1629.7 489.7 %reduce-scatter.34.cloned.1.call-start = ((), (), s32[]{:S(2)}) async-start(), calls=%async_computation.35 | async-start | bytes 1990656 | tf_op jit(solution)/shard_map/reduce_scatter | solution.py:333
  1641.6 660.7 %reduce-scatter.32.cloned.1.call-start = ((), (), s32[]{:S(2)}) async-start(), calls=%async_computation.34 | async-start | bytes 11943936 | tf_op jit(solution)/shard_map/reduce_scatter | solution.py:332
  1655.7 46.7 %copy-start.63 = (f32[2,1024]{1,0:T(2,128)S(1)}, f32[2,1024]{1,0:T(2,128)}, u32[]{:S(2)}) copy-start(f32[2,1024]{1,0:T(2,128)} %get-tuple-element.16) | copy-start | bytes 24580
  1655.7 46.7 %copy-start.64 = (f32[2,1024]{1,0:T(2,128)S(1)}, f32[2,1024]{1,0:T(2,128)}, u32[]{:S(2)}) copy-start(f32[2,1024]{1,0:T(2,128)} %get-tuple-element.23) | copy-start | bytes 24580
  1655.7 57.8 %copy-start.82 = (s32[2,2]{1,0:T(2,128)S(1)}, s32[2,2]{1,0:T(2,128)}, u32[]{:S(2)}) copy-start(s32[2,2]{1,0:T(2,128)} %param.31) | copy-start | bytes 52
  1655.7 59.1 %copy-start.48 = (f32[2,1024]{1,0:T(2,128)S(1)}, f32[2,1024]{1,0:T(2,128)}, u32[]{:S(2)}) copy-start(f32[2,1024]{1,0:T(2,128)} %copy-done.47) | copy-start | bytes 24580
  1655.7 59.1 %copy-start.50 = (f32[2,1024]{1,0:T(2,128)S(1)}, f32[2,1024]{1,0:T(2,128)}, u32[]{:S(2)}) copy-start(f32[2,1024]{1,0:T(2,128)} %copy-done.49) | copy-start | bytes 24580
  1655.7 59.1 %copy-start.60 = (f32[2,288]{1,0:T(2,128)S(1)}, f32[2,288]{1,0:T(2,128)}, u32[]{:S(2)}) copy-start(f32[2,288]{1,0:T(2,128)} %copy-done.59) | copy-start | bytes 6916
  1719.4 582.9 %copy-start.1 = (bf16[101,1152]{1,0:T(8,128)(2,1)S(1)}, bf16[101,1152]{1,0:T(8,128)(2,1)}, u32[]{:S(2)}) copy-start(bf16[101,1152]{1,0:T(8,128)(2,1)} %param.19) | copy-start | bytes 698116
  (67 other events, 279.5 us)
Sparse Core Ops, SparseCore 0:
  10.3 89.7 all-gather.11
  105.2 35.6 all-gather.13
  305.0 75.7 reduce-scatter.15
  382.8 55.0 all-gather.17
  439.8 36.0 all-gather.15
  477.9 55.0 all-gather.19
  535.1 36.0 all-gather.25
  600.6 78.4 reduce-scatter.23
  701.7 38.4 all-gather.27
  803.9 78.3 reduce-scatter.25
  897.6 38.4 all-gather.21
  998.1 78.4 reduce-scatter.19
  1093.5 38.5 all-gather.23
  1134.1 37.4 all-gather.29
  1200.6 78.4 reduce-scatter.27
  1281.5 78.4 reduce-scatter.17
  1362.5 78.4 reduce-scatter.21
  1451.1 37.4 all-gather.31
  1544.8 78.3 reduce-scatter.29
  1627.2 105.6 reduce-scatter.43
  1737.6 103.9 reduce-scatter.41
  1845.6 65.7 reduce-scatter.39
  1915.8 64.9 reduce-scatter.37
  1984.7 65.1 reduce-scatter.35
  2054.3 65.1 reduce-scatter.33
  2123.5 178.7 reduce-scatter.31
where the time goes:
time: 2320 us; the launch traced here: 2310 us
  waiting for transfers between devices  1500 us (65%)
  matrix products  331 us (14%)
  blocking collectives  251 us (11%)
  local copies, waits for them, and re-layouts  139 us (6%)
  other arithmetic  72 us (3%)
    reduce_scatter x4, waiting for transfers between devices, reduce_columns(): lax.psum_scatter(partial_value, 'narrow', scatter_dimension=1, tiled=True)  302 us
    reduce_scatter x4, waiting for transfers between devices, reduce_feature_grads(): lax.psum_scatter(partial_value, 'narrow', scatter_dimension=1, tiled=True)  205 us
    reduce_scatter x1, waiting for transfers between devices, on_device(): lax.psum_scatter(ada_local, 'wide', scatter_dimension=0, tiled=True)  183 us
    all_gather x4, waiting for transfers between devices, spread_grads(): return lax.all_gather(grads_low, 'narrow', axis=1, tiled=True)  140 us
    all_gather x4, waiting for transfers between devices, spread_features(): return lax.all_gather(normed_low, 'narrow', axis=1, tiled=True)  115 us
    reduce_scatter x1, waiting for transfers between devices, on_device(): lax.psum_scatter(up_grad, 'wide', scatter_dimension=0, tiled=True)  109 us
    all_gather x1, waiting for transfers between devices, fetch_rows(): lax.all_gather(ada_weight, 'wide', axis=0, tiled=True)  73.3 us
    reduce_scatter x1, waiting for transfers between devices, on_device(): lax.psum_scatter(out_grad, 'wide', scatter_dimension=1, tiled=True)  69.8 us
  transfers between devices with their start and end apart: 26, of which 24 were waited for; matrix products, arithmetic and copies ran while one was open for 9% of the time, Pallas kernels for 0%

commit v1 on v0

v1 whole, which is shorter than its diff:
```python
import math

import jax
import jax.numpy as jnp
from jax import lax
from jax.experimental import pallas as pl
from jax.experimental.pallas import tpu as pltpu
from jax.sharding import PartitionSpec as P

HEAD_DIM = 72
FRAMES = 16
BLOCK = 128

norm_epsilon = 1e-06
masked_score = -1e30
both = ("narrow", "wide")


def time_embedding(time_ids, full_width):
    half_width = full_width // 2
    frequency = jnp.exp(-math.log(10000.0) * jnp.arange(half_width, dtype=jnp.float32) / half_width)
    angles = time_ids.astype(jnp.float32)[..., None] * frequency
    return jnp.concatenate([jnp.cos(angles), jnp.sin(angles)], axis=-1)


def head_rows(block, head):
    return block[head * HEAD_DIM : (head + 1) * HEAD_DIM].astype(jnp.bfloat16)


def contract(left, right, left_dim, right_dim):
    return lax.dot_general(
        left, right, (((left_dim,), (right_dim,)), ((), ())), preferred_element_type=jnp.float32
    )


def attention_forward_kernel(heads, score_scale, qkv_ref, row_ref, column_ref, out_ref, probs_ref):
    width = heads * HEAD_DIM
    rows_at = lax.broadcasted_iota(jnp.int32, (BLOCK, BLOCK), 0)
    columns_at = lax.broadcasted_iota(jnp.int32, (BLOCK, BLOCK), 1)
    allowed = (rows_at // FRAMES == columns_at // FRAMES) & (
        ((column_ref[...] > 0) & (row_ref[...] > 0)) | (rows_at == columns_at)
    )
    queries = qkv_ref[0, :width].astype(jnp.float32)
    key_rows = qkv_ref[0, width : 2 * width].astype(jnp.float32)
    value_rows = qkv_ref[0, 2 * width :].astype(jnp.float32)
    parts = []
    for head in range(heads):
        scores = (
            contract(head_rows(key_rows, head), head_rows(queries, head), 0, 0) * score_scale
        )
        scores = jnp.where(allowed, scores, masked_score)
        exp_scores = jnp.exp(scores - jnp.max(scores, axis=0, keepdims=True))
        probs = exp_scores * (1.0 / jnp.sum(exp_scores, axis=0, keepdims=True))
        probs_low = probs.astype(jnp.bfloat16)
        probs_ref[0, 0, head] = probs_low
        parts.append(contract(head_rows(value_rows, head), probs_low, 1, 0))
    out_ref[0] = jnp.concatenate(parts, axis=0).astype(jnp.bfloat16)


def attention_backward_kernel(heads, score_scale, qkv_ref, probs_ref, grad_ref, out_ref):
    width = heads * HEAD_DIM
    queries = qkv_ref[0, :width].astype(jnp.float32)
    key_rows = qkv_ref[0, width : 2 * width].astype(jnp.float32)
    value_rows = qkv_ref[0, 2 * width :].astype(jnp.float32)
    grads = grad_ref[0].astype(jnp.float32)
    query_parts, key_parts, value_parts = [], [], []
    for head in range(heads):
        probs_low = probs_ref[0, 0, head]
        grad_head = head_rows(grads, head)
        value_parts.append(contract(grad_head, probs_low, 1, 1))
        grad_probs = contract(head_rows(value_rows, head), grad_head, 0, 0)
        probs = probs_low.astype(jnp.float32)
        crossed = jnp.sum(grad_probs * probs, axis=0, keepdims=True)
        grad_scores = (probs * (grad_probs - crossed)).astype(jnp.bfloat16)
        query_parts.append(contract(head_rows(key_rows, head), grad_scores, 1, 0) * score_scale)
        key_parts.append(contract(head_rows(queries, head), grad_scores, 1, 1) * score_scale)
    out_ref[0] = jnp.concatenate(query_parts + key_parts + value_parts, axis=0).astype(jnp.bfloat16)


def attention_forward(qkv, in_clip):
    panels, triple, tokens = qkv.shape
    heads = triple // (3 * HEAD_DIM)
    blocks = tokens // BLOCK
    return pl.pallas_call(
        lambda *refs: attention_forward_kernel(heads, 1.0 / math.sqrt(HEAD_DIM), *refs),
        grid=(blocks, panels),
        in_specs=[
            pl.BlockSpec((1, triple, BLOCK), lambda b, n: (n, 0, b)),
            pl.BlockSpec((1, BLOCK), lambda b, n: (0, b)),
            pl.BlockSpec((BLOCK, 1), lambda b, n: (b, 0)),
        ],
        out_specs=[
            pl.BlockSpec((1, triple // 3, BLOCK), lambda b, n: (n, 0, b)),
            pl.BlockSpec((1, 1, heads, BLOCK, BLOCK), lambda b, n: (b, n, 0, 0, 0)),
        ],
        out_shape=[
            jax.ShapeDtypeStruct((panels, triple // 3, tokens), jnp.bfloat16),
            jax.ShapeDtypeStruct((blocks, panels, heads, BLOCK, BLOCK), jnp.bfloat16),
        ],
        name="attention_forward",
    )(qkv, in_clip[None, :], in_clip[:, None])


def attention_backward(qkv, probs, grad_attended):
    panels, triple, tokens = qkv.shape
    heads = triple // (3 * HEAD_DIM)
    blocks = tokens // BLOCK
    return pl.pallas_call(
        lambda *refs: attention_backward_kernel(heads, 1.0 / math.sqrt(HEAD_DIM), *refs),
        grid=(blocks, panels),
        in_specs=[
            pl.BlockSpec((1, triple, BLOCK), lambda b, n: (n, 0, b)),
            pl.BlockSpec((1, 1, heads, BLOCK, BLOCK), lambda b, n: (b, n, 0, 0, 0)),
            pl.BlockSpec((1, triple // 3, BLOCK), lambda b, n: (n, 0, b)),
        ],
        out_specs=pl.BlockSpec((1, triple, BLOCK), lambda b, n: (n, 0, b)),
        out_shape=jax.ShapeDtypeStruct((panels, triple, tokens), jnp.bfloat16),
        name="attention_backward",
    )(qkv, probs, grad_attended)


def gather_weight(piece):
    gathered = lax.all_gather(piece, both, axis=0, tiled=False)
    panels = lax.axis_size("narrow")
    return gathered.reshape(panels, -1, piece.shape[1])


def scatter_weight_grad(grad):
    panels = grad.shape[0]
    wide = lax.axis_size("wide")
    pieces = grad.reshape(panels * wide, grad.shape[1] // wide, grad.shape[2])
    return lax.psum_scatter(pieces, both, scatter_dimension=0, tiled=False).astype(jnp.float32)


def to_tokens(local):
    micro_count, seq_count, local_width, seq_tokens = local.shape
    panels = lax.axis_size("narrow")
    cut = local.reshape(micro_count * seq_count, local_width, panels, seq_tokens // panels)
    moved = lax.all_to_all(cut.transpose(2, 1, 0, 3), "narrow", 0, 0, tiled=True)
    return moved.reshape(panels * local_width, -1)


def to_features(whole, micro_count, seq_count):
    panels = lax.axis_size("narrow")
    width, token_count = whole.shape
    seqs = micro_count * seq_count
    cut = whole.reshape(panels, width // panels, seqs, token_count // seqs)
    moved = lax.all_to_all(cut, "narrow", 0, 0, tiled=True)
    return moved.transpose(2, 1, 0, 3).reshape(micro_count, seq_count, width // panels, -1)


def norm_forward(values):
    width = values.shape[0]
    center = jnp.sum(values, axis=0, keepdims=True) / width
    shifted = values - center
    variance = jnp.sum(shifted * shifted, axis=0, keepdims=True) / width
    inverse = lax.rsqrt(variance + norm_epsilon)
    return shifted * inverse, inverse


def norm_backward(grad_hat, normed, inverse):
    width = normed.shape[0]
    totals = jnp.sum(grad_hat, axis=0, keepdims=True) / width
    crossed = jnp.sum(grad_hat * normed, axis=0, keepdims=True) / width
    return inverse * (grad_hat - totals - normed * crossed)


def on_device(
    tokens,
    ada_weight,
    ada_bias,
    class_table,
    query_weight,
    key_weight,
    value_weight,
    out_weight,
    up_weight,
    up_bias,
    down_weight,
    down_bias,
    cotangent,
    clip_frames,
    time_ids,
    class_ids,
):
    micro_count, seq_count, local_width, seq_tokens = tokens.shape
    class_count, full_width = class_table.shape
    panels, wide_count = lax.axis_size("narrow"), lax.axis_size("wide")
    narrow_at, wide_at = lax.axis_index("narrow"), lax.axis_index("wide")
    seqs = micro_count * seq_count
    part_tokens = seq_tokens // panels
    token_count = seqs * part_tokens
    own_rows = ada_weight.shape[0]
    highest = lax.Precision.HIGHEST

    first_piece = jnp.concatenate([query_weight, key_weight, value_weight, out_weight.T], axis=1)
    first_full = gather_weight(first_piece)
    up_full = gather_weight(up_weight)
    down_full = gather_weight(down_weight.T)
    triple = 3 * local_width
    qkv_full = first_full[:, :, :triple]
    out_full = first_full[:, :, triple:]

    class_hot = (class_ids.reshape(seqs)[:, None] == jnp.arange(class_count)[None, :]).astype(
        jnp.bfloat16
    )
    condition = time_embedding(time_ids.reshape(seqs), full_width) + jnp.einsum(
        "sc,cd->sd", class_hot, class_table, preferred_element_type=jnp.float32
    )
    sigmoid_cond = jax.nn.sigmoid(condition)
    cond_act = (condition * sigmoid_cond).astype(jnp.bfloat16)
    silu_slope = sigmoid_cond * (1.0 + condition * (1.0 - sigmoid_cond))
    own_cond = lax.dynamic_slice_in_dim(cond_act, wide_at * own_rows, own_rows, axis=1)
    own_slope = lax.dynamic_slice_in_dim(silu_slope, wide_at * own_rows, own_rows, axis=1)
    mod_part = jnp.einsum(
        "sd,dje->jes", own_cond, ada_weight, preferred_element_type=jnp.float32
    ) + jnp.where(wide_at == 0, ada_bias.astype(jnp.float32), 0.0)[:, :, None]
    mod_parts = lax.all_gather(mod_part, both, axis=0, tiled=False)
    mod_sum = jnp.sum(
        mod_parts.reshape(panels, wide_count, 6, local_width, seqs), axis=1
    )
    modulation = mod_sum.transpose(1, 0, 2, 3).reshape(6, full_width, seqs)

    def spread(vector):
        return jnp.broadcast_to(
            vector[:, :, None], (vector.shape[0], seqs, part_tokens)
        ).reshape(vector.shape[0], token_count)

    def gather_sum(values):
        return jnp.sum(values.reshape(values.shape[0], seqs, part_tokens), axis=2)

    shift_one, scale_one, gate_one, shift_two, scale_two, gate_two = [
        spread(modulation[slot_index]) for slot_index in range(6)
    ]
    frame_at = jnp.arange(part_tokens) % FRAMES
    in_clip = (frame_at[None, :] < clip_frames.reshape(seqs)[:, None]).astype(jnp.int32).reshape(-1)

    residual = to_tokens(tokens).astype(jnp.float32)
    upstream = to_tokens(cotangent).astype(jnp.float32)
    normed_one, inverse_one = norm_forward(residual)
    input_one = (normed_one * (1.0 + scale_one) + shift_one).astype(jnp.bfloat16)
    qkv = jnp.einsum(
        "nde,dt->net", qkv_full, input_one, preferred_element_type=jnp.float32
    ).astype(jnp.bfloat16)
    attended, probs = attention_forward(qkv, in_clip)
    branch = jnp.einsum("nde,net->dt", out_full, attended, preferred_element_type=jnp.float32)
    middle = residual + gate_one * branch
    normed_two, inverse_two = norm_forward(middle)
    input_two = (normed_two * (1.0 + scale_two) + shift_two).astype(jnp.bfloat16)
    up_bias_full = lax.all_gather(up_bias, "narrow", axis=0).astype(jnp.float32)
    down_bias_full = lax.all_gather(down_bias, "narrow", axis=0, tiled=True).astype(jnp.float32)
    up_act = (
        jnp.einsum("nde,dt->net", up_full, input_two, preferred_element_type=jnp.float32)
        + up_bias_full[:, :, None]
    )
    hidden, gelu_back = jax.vjp(lambda v: jax.nn.gelu(v, approximate=True), up_act)
    hidden_low = hidden.astype(jnp.bfloat16)
    slope_low = gelu_back(jnp.ones_like(up_act))[0].astype(jnp.bfloat16)
    mlp_out = (
        jnp.einsum("nde,net->dt", down_full, hidden_low, preferred_element_type=jnp.float32)
        + down_bias_full[:, None]
    )
    output = (middle + gate_two * mlp_out).astype(jnp.bfloat16)
    output_local = to_features(output, micro_count, seq_count)

    grad_gate_two = gather_sum(upstream * mlp_out)
    grad_mlp = (gate_two * upstream).astype(jnp.bfloat16)
    down_bias_part = jnp.sum(grad_mlp.astype(jnp.float32), axis=1)
    down_grad = jnp.einsum(
        "dt,net->nde", grad_mlp, hidden_low, preferred_element_type=jnp.float32
    ).astype(jnp.bfloat16)
    down_grad = scatter_weight_grad(down_grad)
    grad_hidden = jnp.einsum("nde,dt->net", down_full, grad_mlp, preferred_element_type=jnp.float32)
    grad_up = (grad_hidden * slope_low.astype(jnp.float32)).astype(jnp.bfloat16)
    up_bias_part = jnp.sum(grad_up.astype(jnp.float32), axis=2)
    up_grad = jnp.einsum(
        "dt,net->nde", input_two, grad_up, preferred_element_type=jnp.float32
    ).astype(jnp.bfloat16)
    up_grad = scatter_weight_grad(up_grad)
    grad_input_two = jnp.einsum("nde,net->dt", up_full, grad_up, preferred_element_type=jnp.float32)
    grad_shift_two = gather_sum(grad_input_two)
    grad_scale_two = gather_sum(grad_input_two * normed_two)
    grad_middle = upstream + norm_backward(
        grad_input_two * (1.0 + scale_two), normed_two, inverse_two
    )
    grad_gate_one = gather_sum(grad_middle * branch)
    grad_branch = (gate_one * grad_middle).astype(jnp.bfloat16)
    out_grad = jnp.einsum(
        "dt,net->nde", grad_branch, attended, preferred_element_type=jnp.float32
    ).astype(jnp.bfloat16)
    grad_attended = jnp.einsum(
        "nde,dt->net", out_full, grad_branch, preferred_element_type=jnp.float32
    ).astype(jnp.bfloat16)
    grad_qkv = attention_backward(qkv, probs, grad_attended)
    qkv_grad = jnp.einsum(
        "dt,net->nde", input_one, grad_qkv, preferred_element_type=jnp.float32
    ).astype(jnp.bfloat16)
    first_grad = scatter_weight_grad(jnp.concatenate([qkv_grad, out_grad], axis=2))
    grad_input_one = jnp.einsum(
        "nde,net->dt", qkv_full, grad_qkv, preferred_element_type=jnp.float32
    )
    grad_shift_one = gather_sum(grad_input_one)
    grad_scale_one = gather_sum(grad_input_one * normed_one)
    grad_tokens = grad_middle + norm_backward(
        grad_input_one * (1.0 + scale_one), normed_one, inverse_one
    )
    grad_local = to_features(grad_tokens.astype(jnp.bfloat16), micro_count, seq_count)

    mod_part = jnp.stack(
        [
            grad_shift_one,
            grad_scale_one,
            grad_gate_one,
            grad_shift_two,
            grad_scale_two,
            grad_gate_two,
        ]
    )
    mod_grad, up_bias_sum, down_bias_sum = lax.psum((mod_part, up_bias_part, down_bias_part), both)
    own_mod = lax.dynamic_slice_in_dim(mod_grad, narrow_at * local_width, local_width, axis=1)
    up_bias_grad = lax.dynamic_index_in_dim(up_bias_sum, narrow_at, 0, keepdims=False)
    down_bias_grad = lax.dynamic_slice_in_dim(down_bias_sum, narrow_at * local_width, local_width)
    ada_grad = jnp.einsum(
        "sd,jes->dje", own_cond.astype(jnp.float32), own_mod, precision=highest
    )
    ada_bias_grad = jnp.sum(own_mod, axis=2)
    cond_local = own_slope * jnp.einsum(
        "jes,dje->sd", own_mod, ada_weight.astype(jnp.float32), precision=highest
    )
    cond_grad = lax.psum(
        lax.dynamic_update_slice_in_dim(
            jnp.zeros((seqs, full_width), jnp.float32), cond_local, wide_at * own_rows, axis=1
        ),
        both,
    )
    table_grad = jnp.einsum(
        "sc,sd->cd", class_hot.astype(jnp.float32), cond_grad, precision=highest
    )
    return (
        output_local,
        grad_local.astype(jnp.float32),
        ada_grad,
        ada_bias_grad,
        table_grad,
        first_grad[:, :local_width],
        first_grad[:, local_width : 2 * local_width],
        first_grad[:, 2 * local_width : triple],
        first_grad[:, triple:].T,
        up_grad,
        up_bias_grad,
        down_grad.T,
        down_bias_grad,
    )


def solution(mesh):
    return jax.shard_map(
        on_device,
        mesh=mesh,
        in_specs=(
            P(None, None, "narrow", "wide"),
            P("wide", None, "narrow"),
            P(None, "narrow"),
            P(),
            P("wide", "narrow"),
            P("wide", "narrow"),
            P("wide", "narrow"),
            P("narrow", "wide"),
            P("wide", "narrow"),
            P("narrow"),
            P("narrow", "wide"),
            P("narrow"),
            P(None, None, "narrow", "wide"),
            P(),
            P(),
            P(),
        ),
        out_specs=(
            P(None, None, "narrow", "wide"),
            P(None, None, "narrow", "wide"),
            P("wide", None, "narrow"),
            P(None, "narrow"),
            P(),
            P("wide", "narrow"),
            P("wide", "narrow"),
            P("wide", "narrow"),
            P("narrow", "wide"),
            P("wide", "narrow"),
            P("narrow"),
            P("narrow", "wide"),
            P("narrow"),
        ),
        check_vma=False,
    )
```

time: 2320 us -> 1060 us (0.46)
  waiting for transfers between devices: 1500 us -> 421 us
  matrix products: 331 us -> 207 us
  blocking collectives: 251 us -> 156 us
  Pallas kernels: 0 us -> 58.5 us
  local copies, waits for them, and re-layouts: 139 us -> 111 us
    reduce_scatter x15 -> x3, waiting for transfers between devices: 1090 us -> 351 us  [scatter_weight_grad(): lax.psum_scatter(pieces, both, scatter_dimension=0, tiled=False)]
    all_gather x11 -> x3, waiting for transfers between devices: 409 us -> 22.6 us  [gather_weight(): gathered = lax.all_gather(piece, both, axis=0, tiled=False)]
    dot_general x54 -> x17, matrix products: 331 us -> 207 us  [the longest x1 26.8 us: on_device(): jnp.einsum('nde,dt->net', down_full, grad_mlp, preferred_element_type=jnp...]
    pallas_call x0 -> x2, Pallas kernels: none -> 58.5 us  [the longest x1 33.5 us: attention_backward(): pl.pallas_call(lambda *refs: attention_backward_kernel(heads, 1.0 / math....]
    psum x8 -> x1, blocking collectives: 114 us -> 55.9 us  [on_device(): lax.psum(lax.dynamic_update_slice_in_dim(jnp.zeros((seqs, full_width), jn...]
    all_to_all x0 -> x4, waiting for transfers between devices: none -> 44.9 us  [the longest x2 24.2 us: to_tokens(): lax.all_to_all(cut.transpose(2, 1, 0, 3), 'narrow', 0, 0, tiled=True)]
    all_gather x4 -> x2, blocking collectives: 137 us -> 92.5 us  [the longest x1 87.3 us: on_device(): mod_parts = lax.all_gather(mod_part, both, axis=0, tiled=False)]
    reshape x16 -> x6, local copies, waits for them, and re-layouts: 73.8 us -> 30.2 us  [the longest x3 13.4 us: to_tokens(): local.reshape(micro_count * seq_count, local_width, panels, seq_tokens //...]
  transfers between devices with their start and end apart: 26 -> 11, of which waited for: 24 -> 7; matrix products, arithmetic and copies ran while one was open for 9% -> 22% of each run, Pallas kernels for 0% -> 2%
where the time goes in v1:
time: 1060 us; the launch traced here: 1050 us
  waiting for transfers between devices  421 us (40%)
  matrix products  207 us (20%)
  blocking collectives  156 us (15%)
  local copies, waits for them, and re-layouts  111 us (10%)
  other arithmetic  60.8 us (6%)
  Pallas kernels  58.5 us (6%)
  starting transfers between devices  17.2 us (2%)
  between operations  15.6 us (1%)
    reduce_scatter x3, waiting for transfers between devices, scatter_weight_grad(): lax.psum_scatter(pieces, both, scatter_dimension=0, tiled=False)  351 us
    all_gather x1, blocking collectives, on_device(): mod_parts = lax.all_gather(mod_part, both, axis=0, tiled=False)  87.3 us
    psum x1, blocking collectives, on_device(): lax.psum(lax.dynamic_update_slice_in_dim(jnp.zeros((seqs, full_width), jn...  55.9 us
    pallas_call x1, Pallas kernels, attention_backward(): pl.pallas_call(lambda *refs: attention_backward_kernel(heads, 1.0 / math....  33.5 us
    dot_general x1, matrix products, on_device(): jnp.einsum('nde,dt->net', down_full, grad_mlp, preferred_element_type=jnp...  26.8 us
    pallas_call x1, Pallas kernels, attention_forward(): pl.pallas_call(lambda *refs: attention_forward_kernel(heads, 1.0 / math.s...  25 us
    all_to_all x2, waiting for transfers between devices, to_tokens(): lax.all_to_all(cut.transpose(2, 1, 0, 3), 'narrow', 0, 0, tiled=True)  24.2 us
    dot_general x1, matrix products, on_device(): jnp.einsum('nde,net->dt', down_full, hidden_low, preferred_element_type=j...  23.7 us
  transfers between devices with their start and end apart: 11, of which 7 were waited for; matrix products, arithmetic and copies ran while one was open for 22% of the time, Pallas kernels for 2%

profile of v1, /device:TPU:0, one launch (start us, length us, event | category | flops | bytes accessed | tf_op | source)
XLA Modules:
  0.0 1047.4 jit_solution(49483674106574)
XLA Ops:
  10.8 4.5 reshape.296
  15.4 3.2 copy.219
  18.6 4.2 all-to-all-start
  23.0 5.7 reshape.307
  28.7 3.4 copy.167
  33.9 24.2 %all-to-all-done = bf16[4,288,4,256]{3,2,1,0:T(4,128)(2,1)S(1)} async-done(((bf16[4,288,4,256]{3,2,1,0:T(4,128)(2,1)}), bf16[4,288,4,256]{3,2,1,0:T(4,128)(2,1)S(1)}, u32[]{:S(2)}, u32[]{:S(2)}) %all-to-all-start) | async-done | bytes 2359328 | tf_op jit(solution)/shard_map/all_to_all | solution.py:139
  58.1 4.5 all-to-all-start.2
  62.6 87.3 %all-gather = f32[192,288,4]{1,2,0:T(4,128)} all-gather(f32[6,288,4]{1,2,0:T(4,128)S(1)} %fusion.47), channel_id=2, replica_groups=mesh['wide'=8,'narrow'=4] {'narrow','wide'}, dimensions={0}, use_global_device_ids=true | all-gather | bytes 912384 | tf_op jit(solution)/shard_map/all_gather | solution.py:218
  153.8 5.2 all-gather.5
  160.7 7.7 all-reduce
  174.1 6.1 copy.160
  180.3 4.8 copy_convert_fusion
  185.1 6.8 copy.201
  197.2 7.8 reshape.361
  205.0 3.4 fusion.21
  208.5 16.0 %fusion.15.refs_0_ = bf16[4,864,1024]{2,1,0:T(8,128)(2,1)} fusion(bf16[4,1152,1152]{2,1,0:T(8,128)(2,1)} %bitcast.291, bf16[1152,1024]{0,1:T(8,128)(2,1)S(1)} %fusion.21), kind=kOutput, calls=%fused_computation.34 | convolution fusion | flops 8157265920 | bytes 17694720 | tf_op jit(solution)/shard_map/nde,dt->net/dot_general | solution.py:242
  224.5 25.0 %attention_forward.1 = (bf16[4,288,1024]{2,1,0:T(8,128)(2,1)}, bf16[8,4,4,128,128]{4,3,2,1,0:T(8,128)(2,1)}) custom-call(bf16[4,864,1024]{2,1,0:T(8,128)(2,1)} %fusion.15.refs_0_, s32[1,1024]{1,0:T(1,128)} %bitcast.307, s32[1024,1]{1,0:T(8,128)} %bitcast.290), custom_call_target="tpu_custom_call" | custom-call | tf_op jit(solution)/shard_map/attention_forward/pallas_call | solution.py:84
  249.5 11.4 %fusion.62 = (f32[1024]{0:T(1024)S(1)}, f32[1152,1024]{0,1:T(8,128)S(1)}, f32[1152,1024,1]{0,1,2:T(8,128)}) fusion(f32[1152,1024]{0,1:T(8,128)} %copy.160, f32[1152,4]{0,1:T(4,128)S(1)} %broadcast_in_dim.31, bf16[4,288,1024]{2,1,0:T(8,128)(2,1)} %get-tuple-element.15, bf16[4,1152,1152]{2,1,0:T(8,128)(2,1)} %bitcast.292), kind=kOutput, calls=%fused_computation.134 | convolution fusion | flops 2721446912 | bytes 20076544 | tf_op jit(solution)/shard_map/nde,net->dt/dot_general | solution.py:246
  264.4 19.6 %convolution_add_fusion = f32[1024,4,1152]{2,0,1:T(8,128)} fusion(bf16[4,1152,1152]{2,1,0:T(8,128)(2,1)} %bitcast.281, f32[4,1152]{1,0:T(4,128)S(1)} %bitcast.308, bf16[1152,1024]{0,1:T(8,128)(2,1)S(1)} %fusion.26), kind=kOutput, calls=%fused_computation.4 | convolution fusion | flops 10876354560 | bytes 31868928 | tf_op jit(solution)/shard_map/nde,dt->net/dot_general | solution.py:253
  284.0 22.6 %all-gather.14.cloned.1.call-done = bf16[4608,1152]{1,0:T(8,128)(2,1)} async-done(((bf16[144,1152]{1,0:T(8,128)(2,1)}), bf16[4608,1152]{1,0:T(8,128)(2,1)}) %all-gather.14.cloned.1.call-update) | async-done | bytes 10616848 | tf_op jit(solution)/shard_map/all_gather | solution.py:123
  306.6 23.7 %fusion.60 = f32[1024,1152,1]{1,0,2:T(8,128)} fusion(bf16[4,1152,1152]{2,1,0:T(8,128)(2,1)} %bitcast.309, f32[1024,4,1152]{2,0,1:T(8,128)} %convolution_add_fusion), kind=kOutput, calls=%fused_computation.133 | convolution fusion | flops 10914103296 | bytes 34209792 | tf_op jit(solution)/shard_map/nde,net->dt/dot_general | solution.py:260
  330.2 26.8 %convert_reduce_fusion = (f32[4,1152]{1,0:T(4,128)}, bf16[4,1152,1024]{1,2,0:T(8,128)(2,1)}) fusion(f32[1024,4,1152]{2,0,1:T(8,128)} %convolution_add_fusion, bf16[1152,1024,1]{0,1,2:T(8,128)(2,1)S(1)} %bitcast.289, bf16[4,1152,1152]{2,1,0:T(8,128)(2,1)} %bitcast.310), kind=kOutput, calls=%fused_computation.18 | convolution fusion | flops 10980159488 | bytes 41306112 | tf_op jit(solution)/shard_map/nde,dt->net/dot_general | solution.py:273
  357.0 20.7 %fusion.29 = (f32[1024]{0:T(1024)S(1)}, f32[1024]{0:T(1024)S(1)}, bf16[1152,1024]{0,1:T(8,128)(2,1)}, bf16[1152,1024]{0,1:T(8,128)(2,1)}, f32[1024,1152,1]{1,0,2:T(8,128)}) fusion(f32[1152,4]{0,1:T(4,128)S(1)} %add.158, f32[1024]{0:T(1024)S(1)} %add_rsqrt_fusion, f32[1152,1024]{0,1:T(8,128)S(1)} %bitcast.273, f32[1024]{0:T(1024)S(1)} %broadcast_multiply_fusion.4, ...), kind=kOutput, calls=%fused_computation.67 | convolution fusion | flops 10885789696 | bytes 43704832 | tf_op jit(solution)/shard_map/nde,net->dt/dot_general | solution.py:280
  377.7 8.4 bitcast_reduce_fusion.2
  386.5 10.9 %fusion.42.refs_2_ = bf16[4,288,1024]{2,1,0:T(8,128)(2,1)} fusion(bf16[1152,1024]{0,1:T(8,128)(2,1)S(1)} %fusion.19, bf16[4,1152,1152]{2,1,0:T(8,128)(2,1)} %bitcast.293), kind=kOutput, calls=%fused_computation.85 | convolution fusion | flops 2719088640 | bytes 8257536 | tf_op jit(solution)/shard_map/nde,dt->net/dot_general | solution.py:291
  397.5 4.5 fusion.30
  402.0 33.5 %attention_backward.1 = bf16[4,864,1024]{2,1,0:T(8,128)(2,1)} custom-call(bf16[4,864,1024]{2,1,0:T(8,128)(2,1)} %fusion.15.refs_0_, bf16[8,4,4,128,128]{4,3,2,1,0:T(8,128)(2,1)} %get-tuple-element.16.refs_1_, bf16[4,288,1024]{2,1,0:T(8,128)(2,1)} %fusion.42.refs_2_), custom_call_target="tpu_custom_call" | custom-call | tf_op jit(solution)/shard_map/attention_backward/pallas_call | solution.py:108
  435.5 14.4 %fusion.10 = bf16[4,1152,864]{1,2,0:T(8,128)(2,1)} fusion(bf16[4,864,1024]{2,1,0:T(8,128)(2,1)} %attention_backward.1, bf16[1152,1024]{0,1:T(8,128)(2,1)} %copy-done.10), kind=kOutput, calls=%fused_computation.21 | convolution fusion | flops 8157708288 | bytes 17399808 | tf_op jit(solution)/shard_map/dt,net->nde/dot_general | solution.py:295
  450.0 17.5 %fusion.28 = (f32[1024]{0:T(1024)}, f32[1024]{0:T(1024)}, f32[1152,1024,1]{0,1,2:T(8,128)}) fusion(f32[1152,4]{0,1:T(4,128)S(1)} %copy-done.12, f32[1024]{0:T(1024)S(1)} %bitcast.299, f32[1152,1024]{0,1:T(8,128)S(1)} %bitcast.275, f32[1024]{0:T(1024)S(1)} %bitcast.303, bf16[4,864,1024]{2,1,0:T(8,128)(2,1)} %attention_backward.1, ...), kind=kOutput, calls=%fused_computation.66 | convolution fusion | flops 8160802816 | bytes 24807424 | tf_op jit(solution)/shard_map/nde,net->dt/dot_general | solution.py:299
  467.5 3.1 bitcast_reduce_fusion.3
  476.7 8.7 pad_maximum_fusion
  485.5 15.5 %copy.178 = bf16[4,1152,1152]{2,1,0:T(8,128)(2,1)} copy(bf16[4,1152,1152]{1,2,0:T(8,128)(2,1)} %pad_maximum_fusion) | data formatting | bytes 21233664 | tf_op jit(solution)/shard_map/concatenate | solution.py:298
  502.6 18.6 %convolution_convert_fusion = bf16[4,1152,1152]{1,2,0:T(8,128)(2,1)} fusion(bf16[1152,1024]{0,1:T(8,128)(2,1)S(1)} %copy-done.5, f32[1024,4,1152]{2,0,1:T(8,128)} %convolution_add_fusion), kind=kOutput, calls=%fused_computation | convolution fusion | flops 10919411712 | bytes 31850496 | tf_op jit(solution)/shard_map/dt,net->nde/dot_general | solution.py:269
  522.9 17.4 %convolution_convert_fusion.1 = bf16[4,1152,1152]{1,2,0:T(8,128)(2,1)} fusion(bf16[4,1152,1024]{1,2,0:T(8,128)(2,1)} %get-tuple-element.53, bf16[1152,1024]{0,1:T(8,128)(2,1)S(1)} %copy-done.9), kind=kOutput, calls=%fused_computation.1 | convolution fusion | flops 10876944384 | bytes 22413312 | tf_op jit(solution)/shard_map/dt,net->nde/dot_general | solution.py:276
  541.1 6.0 add_convert_fusion
  549.5 5.7 reshape.308
  555.3 4.5 all-to-all-start.3
  562.3 5.6 reshape.305
  567.9 20.7 %all-to-all-done.3 = bf16[4,288,4,256]{3,2,1,0:T(4,128)(2,1)} async-done(((bf16[4,288,4,256]{3,2,1,0:T(4,128)(2,1)}), bf16[4,288,4,256]{3,2,1,0:T(4,128)(2,1)}, u32[]{:S(2)}, u32[]{:S(2)}) %all-to-all-start.3) | async-done | bytes 2359328 | tf_op jit(solution)/shard_map/all_to_all | solution.py:148
  588.6 3.6 all-to-all-start.1
  597.7 55.9 %all-reduce.1 = (f32[4,1152]{1,0:T(4,128)S(1)}, f32[4,1152]{1,0:T(4,128)S(1)}, f32[1152]{0:T(1024)S(1)}) all-reduce(f32[4,1152]{1,0:T(4,128)S(1)} %dynamic_update_slice.3, f32[4,1152]{1,0:T(4,128)S(1)} %copy-done.23, f32[1152]{0:T(1024)S(1)} %reduce_sum.182), channel_id=1, replica_groups=mesh['wide'=8,'narrow'=4] {'narrow','wide'}, use_global_device_ids=true, to_apply=%region_17.18 | all-reduce | flops 10368 | bytes 82944 | tf_op jit(solution)/shard_map/psum | solution.py:330
  662.6 5.3 copy.174
  667.8 6.8 reshape.323
  674.6 3.3 copy.166
  677.9 5.4 reshape.306
  683.3 61.2 %reduce-scatter.4.cloned.1.call-done = bf16[1,144,1152]{2,1,0:T(8,128)(2,1)} async-done(((bf16[32,144,1152]{2,1,0:T(8,128)(2,1)}), bf16[1,144,1152]{2,1,0:T(8,128)(2,1)}) %reduce-scatter.4.cloned.1.call-update) | async-done | bytes 331792 | tf_op jit(solution)/shard_map/reduce_scatter | solution.py:132
  746.6 144.9 %reduce-scatter.8.cloned.1.call-done = bf16[1,144,1152]{2,1,0:T(8,128)(2,1)} async-done(((bf16[32,144,1152]{2,1,0:T(8,128)(2,1)}), bf16[1,144,1152]{2,1,0:T(8,128)(2,1)}) %reduce-scatter.8.cloned.1.call-update) | async-done | bytes 331792 | tf_op jit(solution)/shard_map/reduce_scatter | solution.py:132
  893.4 145.1 %reduce-scatter.6.cloned.1.call-done = bf16[1,144,1152]{2,1,0:T(8,128)(2,1)} async-done(((bf16[32,144,1152]{2,1,0:T(8,128)(2,1)}), bf16[1,144,1152]{2,1,0:T(8,128)(2,1)}) %reduce-scatter.6.cloned.1.call-update) | async-done | bytes 331792 | tf_op jit(solution)/shard_map/reduce_scatter | solution.py:132
  (183 shorter events, 60.7 us)
Async XLA Ops:
  7.2 26.6 %copy-start = (bf16[144,6,288]{2,0,1:T(8,128)(2,1)S(1)}, bf16[144,6,288]{2,0,1:T(8,128)(2,1)}, u32[]{:S(2)}) copy-start(bf16[144,6,288]{2,0,1:T(8,128)(2,1)} %param.17) | copy-start | bytes 1492996
  7.2 201.3 %all-gather.10.cloned.1.call-start = ((), (), s32[]{:S(2)}) async-start(), calls=%async_computation.11 | async-start | bytes 10948608 | tf_op jit(solution)/shard_map/all_gather | solution.py:123
  9.3 255.0 %all-gather.12.cloned.1.call-start = ((), (), s32[]{:S(2)}) async-start(), calls=%async_computation.12 | async-start | bytes 10948608 | tf_op jit(solution)/shard_map/all_gather | solution.py:123
  10.1 296.5 %all-gather.14.cloned.1.call-start = ((), (), s32[]{:S(2)}) async-start(), calls=%async_computation.13 | async-start | bytes 10948608 | tf_op jit(solution)/shard_map/all_gather | solution.py:123
  15.3 7.5 copy-start.30
  15.3 7.6 copy-start.35
  18.6 39.5 %all-to-all-start = ((bf16[4,288,4,256]{3,2,1,0:T(4,128)(2,1)}), bf16[4,288,4,256]{3,2,1,0:T(4,128)(2,1)S(1)}, u32[]{:S(2)}, u32[]{:S(2)}) async-start(bf16[4,288,4,256]{3,2,1,0:T(4,128)(2,1)} %bitcast.286), calls=%async_computation | async-start | bytes 4718592 | tf_op jit(solution)/shard_map/all_to_all | solution.py:139
  23.0 9.3 copy-start.32
  23.0 9.3 copy-start.34
  23.0 10.2 copy-start.24
  32.1 120.2 %copy-start.36 = (s32[2,2]{1,0:T(2,128)S(1)}, s32[2,2]{1,0:T(2,128)}, u32[]{:S(2)}) copy-start(s32[2,2]{1,0:T(2,128)} %param.29) | copy-start | bytes 52
  32.5 121.3 %copy-start.25 = (bf16[1152]{0:T(1024)(128)(2,1)S(1)}, bf16[1152]{0:T(1024)(128)(2,1)}, u32[]{:S(2)}) copy-start(bf16[1152]{0:T(1024)(128)(2,1)} %param.25) | copy-start | bytes 6916
  33.7 125.4 %copy-start.37 = (u32[32]{0:T(128)S(1)}, u32[32]{0:T(128)}, u32[]{:S(2)}) copy-start(u32[32]{0:T(128)} %constant.73) | copy-start | bytes 388
  33.7 126.7 %copy-start.31 = (bf16[288]{0:T(512)(128)(2,1)S(1)}, bf16[288]{0:T(512)(128)(2,1)}, u32[]{:S(2)}) copy-start(bf16[288]{0:T(512)(128)(2,1)} %param.27) | copy-start | bytes 1732
  58.1 122.2 %all-to-all-start.2 = ((bf16[4,288,4,256]{3,1,2,0:T(8,128)(2,1)}), bf16[4,288,4,256]{3,1,2,0:T(8,128)(2,1)}, u32[]{:S(2)}, u32[]{:S(2)}) async-start(bf16[4,288,4,256]{3,1,2,0:T(8,128)(2,1)} %copy.167), calls=%async_computation.2 | async-start | bytes 4718592 | tf_op jit(solution)/shard_map/all_to_all | solution.py:139
  62.6 533.4 %all-reduce.4.cloned.1.call-start = ((), (), s32[]{:S(2)}) async-start(), calls=%async_computation.7 | async-start | bytes 221184 | tf_op jit(solution)/shard_map/psum | solution.py:319
  152.2 52.8 %copy-start.11 = (f32[1152,4]{0,1:T(4,128)}, f32[1152,4]{0,1:T(4,128)S(1)}, u32[]{:S(2)}) copy-start(f32[1152,4]{0,1:T(4,128)S(1)} %add.151) | copy-start | bytes 55300
  152.5 21.7 %copy-start.20 = (s32[1,1,4,256]{3,1,2,0:T(1,128)}, s32[1,1,4,256]{3,1,2,0:T(1,128)S(1)}, u32[]{:S(2)}) copy-start(s32[1,1,4,256]{3,1,2,0:T(1,128)S(1)} %copy.211) | copy-start | bytes 12292
  171.2 33.8 %copy-start.15 = (f32[1,2,4,128]{3,1,2,0:T(2,128)}, f32[1,2,4,128]{3,1,2,0:T(2,128)S(1)}, u32[]{:S(2)}) copy-start(f32[1,2,4,128]{3,1,2,0:T(2,128)S(1)} %copy.210) | copy-start | bytes 12292
  180.2 24.8 %copy-start.17 = (f32[1,2,4,128]{3,1,2,0:T(2,128)}, f32[1,2,4,128]{3,1,2,0:T(2,128)S(1)}, u32[]{:S(2)}) copy-start(f32[1,2,4,128]{3,1,2,0:T(2,128)S(1)} %copy.209) | copy-start | bytes 12292
  208.5 16.0 %copy-start.10 = (bf16[1152,1024]{0,1:T(8,128)(2,1)}, bf16[1152,1024]{0,1:T(8,128)(2,1)S(1)}, u32[]{:S(2)}) copy-start(bf16[1152,1024]{0,1:T(8,128)(2,1)S(1)} %fusion.21) | copy-start | bytes 7077892
  260.9 2.3 copy-start.1
  264.3 19.6 %copy-start.8 = (bf16[1152,1024]{0,1:T(8,128)(2,1)}, bf16[1152,1024]{0,1:T(8,128)(2,1)S(1)}, u32[]{:S(2)}) copy-start(bf16[1152,1024]{0,1:T(8,128)(2,1)S(1)} %fusion.26) | copy-start | bytes 7077892
  306.6 23.7 %copy-start.7 = (bf16[1152,4,256]{0,2,1:T(8,128)(2,1)S(1)}, bf16[1152,4,256]{0,2,1:T(8,128)(2,1)}, u32[]{:S(2)}) copy-start(bf16[1152,4,256]{0,2,1:T(8,128)(2,1)} %copy.170) | copy-start | bytes 7077892
  306.6 50.5 %slice-start = ((s8[4718592]{0:T(1024)(128)(4,1)}), s8[524288]{0:T(1024)(128)(4,1)S(1)}, s32[]{:S(2)}) async-start(s8[4718592]{0:T(1024)(128)(4,1)} %bitcast.272), calls=%async_computation.14 | async-start | bytes 1048576
  330.2 26.8 %slice-start.1 = ((s8[4718592]{0:T(1024)(128)(4,1)}), s8[4194304]{0:T(1024)(128)(4,1)S(1)}, s32[]{:S(2)}) async-start(s8[4718592]{0:T(1024)(128)(4,1)} %bitcast.272), calls=%async_computation.15 | async-start | bytes 8388608
  386.1 11.4 %copy-start.2 = (f32[1152,1024]{0,1:T(8,128)}, f32[1152,1024]{0,1:T(8,128)S(1)}, u32[]{:S(2)}) copy-start(f32[1152,1024]{0,1:T(8,128)S(1)} %get-tuple-element.25) | copy-start | bytes 14155780
  386.5 11.0 %copy-start.6 = (bf16[4,288,1024]{2,1,0:T(8,128)(2,1)S(1)}, bf16[4,288,1024]{2,1,0:T(8,128)(2,1)}, u32[]{:S(2)}) copy-start(bf16[4,288,1024]{2,1,0:T(8,128)(2,1)} %get-tuple-element.15) | copy-start | bytes 7077892
  402.0 47.9 %slice-start.2 = ((s8[4718592]{0:T(1024)(128)(4,1)}), s8[524288]{0:T(1024)(128)(4,1)S(1)}, s32[]{:S(2)}) async-start(s8[4718592]{0:T(1024)(128)(4,1)} %bitcast.274), calls=%async_computation.16 | async-start | bytes 1048576
  435.5 14.4 %slice-start.3 = ((s8[4718592]{0:T(1024)(128)(4,1)}), s8[4194304]{0:T(1024)(128)(4,1)S(1)}, s32[]{:S(2)}) async-start(s8[4718592]{0:T(1024)(128)(4,1)} %bitcast.274), calls=%async_computation.17 | async-start | bytes 8388608
  435.5 14.4 %copy-start.12 = (f32[1152,4]{0,1:T(4,128)S(1)}, f32[1152,4]{0,1:T(4,128)}, u32[]{:S(2)}) copy-start(f32[1152,4]{0,1:T(4,128)} %copy-done.11) | copy-start | bytes 55300
  435.5 14.4 %copy-start.16 = (f32[1,2,4,128]{3,1,2,0:T(2,128)S(1)}, f32[1,2,4,128]{3,1,2,0:T(2,128)}, u32[]{:S(2)}) copy-start(f32[1,2,4,128]{3,1,2,0:T(2,128)} %copy-done.15) | copy-start | bytes 12292
  435.5 14.4 %copy-start.18 = (f32[1,2,4,128]{3,1,2,0:T(2,128)S(1)}, f32[1,2,4,128]{3,1,2,0:T(2,128)}, u32[]{:S(2)}) copy-start(f32[1,2,4,128]{3,1,2,0:T(2,128)} %copy-done.17) | copy-start | bytes 12292
  470.6 6.1 copy-start.4
  476.7 267.9 %reduce-scatter.4.cloned.1.call-start = ((), (), s32[]{:S(2)}) async-start(), calls=%async_computation.8 | async-start | bytes 10948608 | tf_op jit(solution)/shard_map/reduce_scatter | solution.py:132
  500.9 1.7 copy-start.5
  501.0 390.6 %reduce-scatter.8.cloned.1.call-start = ((), (), s32[]{:S(2)}) async-start(), calls=%async_computation.10 | async-start | bytes 10948608 | tf_op jit(solution)/shard_map/reduce_scatter | solution.py:132
  521.2 1.7 copy-start.9
  521.3 517.2 %reduce-scatter.6.cloned.1.call-start = ((), (), s32[]{:S(2)}) async-start(), calls=%async_computation.9 | async-start | bytes 10948608 | tf_op jit(solution)/shard_map/reduce_scatter | solution.py:132
  540.3 0.7 copy-start.26
  540.3 0.7 copy-start.19
  549.5 10.3 copy-start.3
  555.3 33.3 %all-to-all-start.3 = ((bf16[4,288,4,256]{3,2,1,0:T(4,128)(2,1)}), bf16[4,288,4,256]{3,2,1,0:T(4,128)(2,1)}, u32[]{:S(2)}, u32[]{:S(2)}) async-start(bf16[4,288,4,256]{3,2,1,0:T(4,128)(2,1)} %reshape.308), calls=%async_computation.3 | async-start | bytes 4718592 | tf_op jit(solution)/shard_map/all_to_all | solution.py:148
  562.3 30.0 %copy-start.14 = (f32[4,288,4]{1,2,0:T(4,128)S(1)}, f32[4,288,4]{1,2,0:T(4,128)}, u32[]{:S(2)}) copy-start(f32[4,288,4]{1,2,0:T(4,128)} %get-tuple-element.35) | copy-start | bytes 55300
  567.9 29.8 %copy-start.23 = (f32[4,1152]{1,0:T(4,128)S(1)}, f32[4,1152]{1,0:T(4,128)}, u32[]{:S(2)}) copy-start(f32[4,1152]{1,0:T(4,128)} %get-tuple-element.52) | copy-start | bytes 55300
  567.9 88.5 %copy-start.33 = (s32[4]{0:T(128)S(1)}, s32[4]{0:T(128)}, u32[]{:S(2)}) copy-start(s32[4]{0:T(128)} %copy-done.32) | copy-start | bytes 52
  567.9 89.7 %copy-start.22 = (bf16[4,144,1]{1,0,2:T(4,128)(2,1)S(1)}, bf16[4,144,1]{1,0,2:T(4,128)(2,1)}, u32[]{:S(2)}) copy-start(bf16[4,144,1]{1,0,2:T(4,128)(2,1)} %copy-done.21) | copy-start | bytes 3460
  588.6 86.0 %all-to-all-start.1 = ((bf16[4,288,4,256]{3,2,1,0:T(4,128)(2,1)}), bf16[4,288,4,256]{3,2,1,0:T(4,128)(2,1)S(1)}, u32[]{:S(2)}, u32[]{:S(2)}) async-start(bf16[4,288,4,256]{3,2,1,0:T(4,128)(2,1)} %reshape.305), calls=%async_computation.1 | async-start | bytes 4718592 | tf_op jit(solution)/shard_map/all_to_all | solution.py:148
  (5 other events, 3.1 us)
Sparse Core Ops, SparseCore 0:
  11.6 113.3 all-gather.9
  127.9 89.4 all-gather.11
  220.4 86.1 all-gather.13
  476.8 119.1 all-reduce.3
  601.9 142.5 reduce-scatter.3
  750.5 141.0 reduce-scatter.7
  897.6 140.8 reduce-scatter.5
